TPU v7x, 32 devices: a whole 2x2x4 slice. The times are simulated.
32 devices in a mesh: seq: 4 (over y, x), tensor: 8 (over z, core).
Axes of the slice: x: 2, y: 2, z: 4, core: 2. Of those that a mesh axis runs over, the one named last changes fastest.
Arguments:
- hidden_in: bfloat16 [4096, 2304], P(('seq', 'tensor')), may hold values from -6 to 6
- norm_attn: float32 [2304], replicated, may hold values from 0.1 to 1.9
- norm_ffn: float32 [2304], replicated, may hold values from 0.1 to 1.9
- w_qkv: bfloat16 [3, 2304, 512], P(None, None, 'tensor'), may hold values from -1 to 1
- w_out: bfloat16 [512, 2304], P('tensor'), may hold values from -0.25 to 0.25
- w_router: float32 [2304, 8], replicated, may hold values from -4 to 4
- w_gate_up: bfloat16 [2, 23040, 2304], P(None, 'tensor'), may hold values from -0.125 to 0.125
- w_down: bfloat16 [23040, 2304], P('tensor'), may hold values from -0.109375 to 0.109375
- segment_ids: int32 [4096], P('seq'), may hold values from 0 to 7, never falling along the last dimension, each value on 1 to 3072 neighbouring positions
- expert_ids: int32 [4096, 2], P(('seq', 'tensor')), may hold values from 0 to 7, all different within a row; in each aligned block of 128 rows (0 to 127, 128 to 255, ...) at most 64 rows name the same one
Outputs:
- hidden_out: bfloat16 [4096, 2304], P(('seq', 'tensor'))
- kv_cache: bfloat16 [8, 4096, 128], P('tensor', 'seq')
Inputs may be any that keep to these rules, and one draw needn't show every extreme that they name: `segment_ids`: nondecreasing along the stream; each prompt has 1 to 3072 tokens and one has exactly 3072. `expert_ids`: the two experts of a token differ. Within each aligned block of 128 tokens (the tokens of one device), no expert is named by more than 64 tokens, a bound that some block reaches.
All inputs are finite; a program needn't handle non-finite values.
Results may differ from a plain program's by a relative error of at most 0.019.
Values may be sent and summed in bfloat16 or wider, within the bound.
A program may use at most 128 MiB of HBM per device.

v0:
```python
import math
import jax
import jax.numpy as jnp
from jax import lax
from jax.sharding import PartitionSpec as P

HD = 64
epsilon = 1e-06
low_score = -1e30


def rms_norm(hidden_rows, gain):
    as_float = hidden_rows.astype(jnp.float32)
    scale = lax.rsqrt(jnp.mean(as_float * as_float, axis=-1, keepdims=True) + epsilon)
    return (as_float * scale * gain).astype(jnp.bfloat16)


def rotate(head_rows, positions):
    half_size = head_rows.shape[-1] // 2
    frequency = jnp.exp(jnp.arange(half_size, dtype=jnp.float32) * (-math.log(10000.0) / half_size))
    angles = positions.astype(jnp.float32)[:, None] * frequency[None, :]
    cosine = jnp.cos(angles)[:, None, :]
    sine_part = jnp.sin(angles)[:, None, :]
    front_half = head_rows[..., :half_size]
    back_half = head_rows[..., half_size:]
    return jnp.concatenate(
        [front_half * cosine - back_half * sine_part, back_half * cosine + front_half * sine_part],
        axis=-1,
    )


def fold_keys(
    softmax_state, query_rows, query_segments, query_positions, kv_rows, key_segments, key_start
):
    running_max, denominator, weighted_sum = softmax_state
    row_count = kv_rows.shape[0]
    block_size = math.gcd(row_count, 2048)
    head_size = query_rows.shape[-1]
    for block_start in range(0, row_count, block_size):
        kv_block = kv_rows[block_start : block_start + block_size]
        key_block = kv_block[..., :head_size]
        value_block = kv_block[..., head_size:]
        segment_block = key_segments[block_start : block_start + block_size]
        position_block = key_start + block_start + jnp.arange(block_size, dtype=jnp.int32)
        scores = (
            jnp.einsum("qhd,khd->hqk", query_rows, key_block, preferred_element_type=jnp.float32)
            * 0.125
        )
        allowed = (query_segments[:, None] == segment_block[None, :]) & (
            position_block[None, :] <= query_positions[:, None]
        )
        masked = jnp.where(allowed[None], scores, low_score)
        new_max = jnp.maximum(running_max, jnp.max(masked, axis=-1))
        weights = jnp.where(allowed[None], jnp.exp(masked - new_max[..., None]), 0.0)
        factor = jnp.exp(running_max - new_max)
        denominator = denominator * factor + jnp.sum(weights, axis=-1)
        weighted_sum = weighted_sum * factor[..., None] + jnp.einsum(
            "hqk,khd->hqd",
            weights.astype(jnp.bfloat16),
            value_block,
            preferred_element_type=jnp.float32,
        )
        running_max = new_max
    return (running_max, denominator, weighted_sum)


def slot_table(token_ids, target, slot_count):
    is_routed = jnp.any(token_ids == target, axis=1).astype(jnp.int32)
    places = jnp.arange(is_routed.shape[0], dtype=jnp.int32)
    slot_rank = (
        jnp.sum(jnp.where(places[None, :] <= places[:, None], is_routed[None, :], 0), axis=1) - 1
    )
    chosen_slot = (is_routed[None, :] == 1) & (
        slot_rank[None, :] == jnp.arange(slot_count, dtype=jnp.int32)[:, None]
    )
    return chosen_slot.astype(jnp.bfloat16)


def expert_apply(slot_rows, slot_ids, own_expert, w_router, w_gate_up, w_down):
    logits = jnp.dot(slot_rows.astype(jnp.float32), w_router, precision=lax.Precision.HIGHEST)
    expert_count = w_router.shape[1]
    one_hot = (
        slot_ids[:, :, None] == jnp.arange(expert_count, dtype=jnp.int32)[None, None, :]
    ).astype(jnp.float32)
    chosen = jnp.sum(one_hot * logits[:, None, :], axis=-1)
    gate_probs = jax.nn.softmax(chosen, axis=-1)
    weight = jnp.sum(jnp.where(slot_ids == own_expert, gate_probs, 0.0), axis=-1)
    contract = (((1,), (1,)), ((), ()))
    gate_act = lax.dot_general(
        slot_rows, w_gate_up[0], contract, preferred_element_type=jnp.float32
    )
    up_act = lax.dot_general(slot_rows, w_gate_up[1], contract, preferred_element_type=jnp.float32)
    hidden_act = (jax.nn.silu(gate_act) * up_act).astype(jnp.bfloat16)
    output = jnp.dot(hidden_act, w_down, preferred_element_type=jnp.float32)
    return (output * weight[:, None]).astype(jnp.bfloat16)


def shards(
    hidden_in,
    norm_attn,
    norm_ffn,
    w_qkv,
    w_out,
    w_router,
    w_gate_up,
    w_down,
    segment_ids,
    expert_ids,
):
    local_rows = hidden_in.shape[0]
    model_width = hidden_in.shape[1]
    tensor_count = lax.axis_size("tensor")
    tensor_place = lax.axis_index("tensor")
    seq_place = lax.axis_index("seq")
    group_rows = local_rows * tensor_count
    head_count = w_qkv.shape[2] // HD
    normed = rms_norm(hidden_in, norm_attn)
    projected = jnp.einsum(
        "td,cdh->tch",
        lax.all_gather(normed, "tensor", axis=0, tiled=True),
        w_qkv,
        preferred_element_type=jnp.float32,
    )
    positions = seq_place * group_rows + jnp.arange(group_rows, dtype=jnp.int32)
    query_rows = rotate(projected[:, 0].reshape(group_rows, head_count, HD), positions).astype(
        jnp.bfloat16
    )
    key_rows = rotate(projected[:, 1].reshape(group_rows, head_count, HD), positions).astype(
        jnp.bfloat16
    )
    value_rows = projected[:, 2].reshape(group_rows, head_count, HD).astype(jnp.bfloat16)
    kv_rows = jnp.concatenate([key_rows, value_rows], axis=-1)
    kv_cache = kv_rows.transpose(1, 0, 2)
    start_state = (
        jnp.full((head_count, group_rows), low_score, jnp.float32),
        jnp.zeros((head_count, group_rows), jnp.float32),
        jnp.zeros((head_count, group_rows, HD), jnp.float32),
    )
    softmax_state = fold_keys(
        start_state,
        query_rows,
        segment_ids,
        positions,
        lax.all_gather(kv_rows, "seq", axis=0, tiled=True),
        lax.all_gather(segment_ids, "seq", axis=0, tiled=True),
        jnp.int32(0),
    )
    running_max, denominator, weighted_sum = softmax_state
    attended = (
        (weighted_sum / denominator[..., None])
        .transpose(1, 0, 2)
        .reshape(group_rows, head_count * HD)
        .astype(jnp.bfloat16)
    )
    attention_sum = lax.psum_scatter(
        jnp.dot(attended, w_out, preferred_element_type=jnp.float32).astype(jnp.bfloat16),
        "tensor",
        scatter_dimension=0,
        tiled=True,
    ).astype(jnp.float32)
    residual = hidden_in.astype(jnp.float32) + attention_sum
    normed_ffn = rms_norm(residual, norm_ffn)
    expert_count = w_router.shape[1]
    slice_count = tensor_count // expert_count
    own_expert = tensor_place // slice_count
    slot_count = local_rows // 2
    full_rows, full_ids = (
        lax.all_gather(normed_ffn, "tensor", axis=0, tiled=True),
        lax.all_gather(expert_ids, "tensor", axis=0, tiled=True),
    )
    block_ids = full_ids.reshape(tensor_count, local_rows, 2)
    slot_tables = jax.vmap(lambda source_ids: slot_table(source_ids, own_expert, slot_count))(
        block_ids
    )
    slot_rows = jnp.einsum(
        "sjr,srd->sjd",
        slot_tables,
        full_rows.reshape(tensor_count, local_rows, model_width),
        preferred_element_type=jnp.float32,
    ).astype(jnp.bfloat16)
    slot_ids = jnp.einsum(
        "sjr,srk->sjk", slot_tables.astype(jnp.float32), block_ids.astype(jnp.float32)
    ).astype(jnp.int32)
    term_rows = expert_apply(
        slot_rows.reshape(-1, model_width),
        slot_ids.reshape(-1, 2),
        own_expert,
        w_router,
        w_gate_up,
        w_down,
    )
    placed = jnp.einsum(
        "sjr,sjd->srd",
        slot_tables,
        term_rows.reshape(tensor_count, slot_count, model_width),
        preferred_element_type=jnp.float32,
    ).reshape(group_rows, model_width)
    expert_sum = lax.psum_scatter(
        placed.astype(jnp.bfloat16), "tensor", scatter_dimension=0, tiled=True
    ).astype(jnp.float32)
    hidden_out = (residual + expert_sum).astype(jnp.bfloat16)
    return (hidden_out, kv_cache)


def solution(mesh):
    placed = (
        P(("seq", "tensor"), None),
        P(),
        P(),
        P(None, None, "tensor"),
        P("tensor", None),
        P(),
        P(None, "tensor", None),
        P("tensor", None),
        P("seq"),
        P(("seq", "tensor"), None),
    )
    return jax.shard_map(
        shards,
        mesh=mesh,
        in_specs=placed,
        out_specs=(P(("seq", "tensor"), None), P("tensor", "seq", None)),
        check_vma=False,
    )
```

profile of v0, /device:TPU:0, one launch (start us, length us, event | category | flops | bytes accessed | tf_op | source)
XLA Modules:
  0.0 339.1 jit_solution(13860457289444476095)
XLA Ops:
  7.2 0.0 copy-start
  7.2 0.0 copy-start.8
  7.2 0.0 all-gather.4.cloned.1.call-start
  7.2 1.3 fusion.20
  8.6 2.1 fusion.22
  10.7 0.0 all-gather.4.cloned.1.call-update
  10.7 0.0 all-gather.6.cloned.1.call-start
  10.8 54.5 %all-gather.4.cloned.1.call-done = bf16[1024,2304]{1,0:T(8,128)(2,1)} async-done(((bf16[128,2304]{1,0:T(8,128)(2,1)}), bf16[1024,2304]{1,0:T(8,128)(2,1)}) %all-gather.4.cloned.1.call-update) | async-done | bytes 4718608 | tf_op jit(solution)/shard_map/all_gather | solution.py:120
  65.3 0.0 copy-done
  65.3 4.0 %fusion.95 = f32[1024,192]{0,1:S(1)} fusion(bf16[1024,2304]{1,0:T(8,128)(2,1)} %all-gather.4.cloned.1.call-done, bf16[2304,192]{0,1:T(8,128)(2,1)S(1)} %bitcast.62), kind=kOutput, calls=%fused_computation.120 | convolution fusion | flops 905969664 | bytes 6389760
  69.3 0.6 fusion.70
  69.9 0.8 fusion.93
  70.6 0.0 all-gather.6.cloned.1.call-update
  70.7 0.0 reduce-scatter.3.cloned.1.call-start
  70.7 0.0 copy-done.8
  70.7 8.1 %all_gather.15 = s32[4096]{0:T(1024)S(1)} all-gather(s32[1024]{0:T(1024)S(1)} %copy-done.8), channel_id=1, replica_groups=mesh['seq'=4,'tensor'=8] {'seq'}, dimensions={0}, use_global_device_ids=true | all-gather | bytes 20480 | tf_op jit(solution)/shard_map/all_gather | solution.py:145
  78.9 17.4 %all-gather.6.cloned.1.call-done = bf16[4096,1,128]{0,2,1:T(8,128)(2,1)} async-done(((bf16[1024,1,128]{0,2,1:T(8,128)(2,1)}), bf16[4096,1,128]{0,2,1:T(8,128)(2,1)}) %all-gather.6.cloned.1.call-update) | async-done | bytes 1048592 | tf_op jit(solution)/shard_map/all_gather | solution.py:144
  96.3 0.0 copy-start.7
  96.3 2.3 fusion.41
  98.6 0.0 copy-done.7
  98.6 4.1 %fusion.8 = (f32[1024]{0:T(1024)S(1)}, f32[1024]{0:T(1024)S(1)}, f32[1024,2048]{1,0:T(8,128)S(1)}) fusion(s32[2048]{0:T(1024)S(1)} %iota_add_fusion, s32[2048]{0:T(1024)S(1)} %get-tuple-element.23, s32[1024]{0:T(1024)S(1)} %iota_add_fusion.1, s32[1024]{0:T(1024)S(1)} %copy-done.8, f32[1024,2048]{1,0:T(8,128)S(1)} %fusion.41, ...), kind=kOutput, calls=%fused_computation.14 | convolution fusion | flops 293861376 | bytes 17211392 | tf_op jit(solution)/shard_map/qhd,khd->hqk/dot_general | solution.py:46
  102.7 0.0 copy-start.4
  102.7 6.2 %fusion.12 = (f32[1024]{0:T(1024)S(1)}, f32[1024]{0:T(1024)S(1)}) fusion(f32[1024,2048]{1,0:T(8,128)S(1)} %fusion.41, f32[1024]{0:T(1024)S(1)} %get-tuple-element.26, s32[2048]{0:T(1024)S(1)} %get-tuple-element.22, s32[1024]{0:T(1024)S(1)} %iota_add_fusion.1, s32[1024]{0:T(1024)S(1)} %copy-done.8, f32[1024]{0:T(1024)S(1)} %get-tuple-element.25, ...), kind=kLoop, calls=%fused_computation.21 | loop fusion | flops 33552384 | bytes 16826368 | tf_op jit(solution)/shard_map/reduce_sum | solution.py:56
  108.9 0.0 copy-done.4
  108.9 0.0 copy-start.11
  108.9 2.8 fusion.29
  111.7 0.0 copy-done.11
  111.7 0.0 copy-start.2
  111.7 8.0 %convolution_convert_fusion.1 = bf16[1024,2304]{1,0:T(8,128)(2,1)} fusion(bf16[64,2304]{1,0:T(8,128)(2,1)S(1)} %copy-done.11, f32[1024,64]{0,1:T(8,128)S(1)} %fusion.29, f32[1024,2048]{1,0:T(8,128)} %copy-done.4, f32[1024]{0:T(1024)S(1)} %get-tuple-element.25, s32[2048]{0:T(1024)S(1)} %iota_add_fusion, s32[2048]{0:T(1024)S(1)} %get-tuple-element.23, ...), kind=kOutput, calls=%fused_computation.17 | convolution fusion | flops 589758464 | bytes 13959168 | tf_op jit(solution)/shard_map/dot_general | solution.py:156
  119.7 0.0 copy-start.9
  119.7 0.0 reduce-scatter.3.cloned.1.call-update
  119.8 0.0 copy-start.6
  119.8 0.2 all-gather.8.cloned.1.call-start
  120.0 54.9 %reduce-scatter.3.cloned.1.call-done = bf16[128,2304]{1,0:T(8,128)(2,1)} async-done(((bf16[1024,2304]{1,0:T(8,128)(2,1)}), bf16[128,2304]{1,0:T(8,128)(2,1)}) %reduce-scatter.3.cloned.1.call-update) | async-done | bytes 589840 | tf_op jit(solution)/shard_map/reduce_scatter | solution.py:155
  174.9 0.0 copy-done.2
  174.9 1.3 multiply_reduce_fusion
  176.2 0.0 copy-done.9
  176.2 2.1 multiply_convert_fusion.1
  178.3 0.0 all-gather.8.cloned.1.call-update
  178.4 0.0 reduce-scatter.5.cloned.1.call-start
  178.4 0.0 copy-done.10
  178.4 9.2 %all_gather.18 = s32[1024,2]{0,1:T(2,128)S(1)} all-gather(s32[128,2]{0,1:T(2,128)S(1)} %copy-done.10), channel_id=1, replica_groups=mesh['seq'=4,'tensor'=8] {'tensor'}, dimensions={0}, use_global_device_ids=true | all-gather | bytes 9216 | tf_op jit(solution)/shard_map/all_gather | solution.py:169
  187.6 0.2 select_reduce_fusion
  187.9 0.2 fusion.77
  188.1 0.1 eq.91
  188.1 40.4 %all-gather.8.cloned.1.call-done = bf16[1024,2304]{1,0:T(8,128)(2,1)} async-done(((bf16[128,2304]{1,0:T(8,128)(2,1)}), bf16[1024,2304]{1,0:T(8,128)(2,1)}) %all-gather.8.cloned.1.call-update) | async-done | bytes 4718608 | tf_op jit(solution)/shard_map/all_gather | solution.py:168
  228.6 3.1 convolution_convert_fusion.2
  231.7 0.0 copy-start.3
  231.7 1.5 copy-done.3
  233.2 0.0 copy-done.6
  233.2 1.9 fusion.96
  235.1 0.1 reduce_sum.80
  235.2 0.1 sub.80
  235.3 12.5 %fusion.2 = f32[512,2880]{0,1:T(8,128)} fusion(bf16[512,2304]{1,0:T(8,128)(2,1)} %bitcast.65, bf16[2,2880,2304]{2,1,0:T(8,128)(2,1)} %param.16), kind=kOutput, calls=%fused_computation.2 | convolution fusion | flops 6794772480 | bytes 21528576 | tf_op jit(solution)/shard_map/dot_general | solution.py:89
  247.8 0.1 div.37
  247.9 0.1 mul.193
  248.0 23.2 %fusion.11 = bf16[512,2304]{1,0:T(8,128)(2,1)} fusion(bf16[2880,2304]{1,0:T(8,128)(2,1)} %param.17, f32[512]{0:T(512)S(1)} %mul.193, f32[512,2880]{0,1:T(8,128)} %fusion.2, bf16[512,2304]{1,0:T(8,128)(2,1)} %bitcast.66, bf16[2,2880,2304]{2,1,0:T(8,128)(2,1)} %param.16), kind=kOutput, calls=%fused_computation.20 | convolution fusion | flops 13600751616 | bytes 37160960 | tf_op jit(solution)/shard_map/dot_general | solution.py:94
  271.2 5.3 %convolution_convert_fusion = bf16[8,128,2304]{2,1,0:T(8,128)(2,1)} fusion(bf16[8,64,2304]{2,1,0:T(8,128)(2,1)} %bitcast.68, s32[8,128]{1,0:T(8,128)S(1)} %broadcast_add_fusion, pred[8,128]{1,0:T(8,128)(4,1)S(1)} %broadcast_compare_fusion), kind=kOutput, calls=%fused_computation.16 | convolution fusion | flops 304480256 | bytes 7083008 | tf_op jit(solution)/shard_map/sjr,sjd->srd/dot_general | solution.py:192
  276.5 0.0 reduce-scatter.5.cloned.1.call-update
  276.6 0.8 copy.26
  277.4 53.1 %reduce-scatter.5.cloned.1.call-done = bf16[128,2304]{1,0:T(8,128)(2,1)} async-done(((bf16[1024,2304]{1,0:T(8,128)(2,1)}), bf16[128,2304]{1,0:T(8,128)(2,1)}) %reduce-scatter.5.cloned.1.call-update) | async-done | bytes 589840 | tf_op jit(solution)/shard_map/reduce_scatter | solution.py:198
  330.5 0.0 copy-done.5
  330.5 2.1 add_convert_fusion
  332.6 0.0 copy-done.1
  (23 shorter events, 0.3 us)
Async XLA Ops:
  7.2 58.1 %copy-start = (bf16[3,2304,64]{1,2,0:T(8,128)(2,1)S(1)}, bf16[3,2304,64]{1,2,0:T(8,128)(2,1)}, u32[]{:S(2)}) copy-start(bf16[3,2304,64]{1,2,0:T(8,128)(2,1)} %param.13) | copy-start | bytes 2654212
  7.2 63.5 %copy-start.8 = (s32[1024]{0:T(1024)S(1)}, s32[1024]{0:T(1024)}, u32[]{:S(2)}) copy-start(s32[1024]{0:T(1024)} %param.18) | copy-start | bytes 12292
  7.2 58.1 %all-gather.4.cloned.1.call-start = ((), (), s32[]{:S(2)}) async-start(), calls=%async_computation.2 | async-start | bytes 5308416 | tf_op jit(solution)/shard_map/all_gather | solution.py:120
  10.7 85.6 %all-gather.6.cloned.1.call-start = ((), (), s32[]{:S(2)}) async-start(), calls=%async_computation.3 | async-start | bytes 1310720 | tf_op jit(solution)/shard_map/all_gather | solution.py:144
  70.7 104.2 %reduce-scatter.3.cloned.1.call-start = ((), (), s32[]{:S(2)}) async-start(), calls=%async_computation.4 | async-start | bytes 5308416 | tf_op jit(solution)/shard_map/reduce_scatter | solution.py:155
  96.3 2.3 copy-start.7
  102.7 6.2 %copy-start.4 = (f32[1024,2048]{1,0:T(8,128)}, f32[1024,2048]{1,0:T(8,128)S(1)}, u32[]{:S(2)}) copy-start(f32[1024,2048]{1,0:T(8,128)S(1)} %get-tuple-element.27) | copy-start | bytes 25165828
  108.9 2.8 copy-start.11
  111.7 63.2 %copy-start.2 = (bf16[128,2304]{1,0:T(8,128)(2,1)S(1)}, bf16[128,2304]{1,0:T(8,128)(2,1)}, u32[]{:S(2)}) copy-start(bf16[128,2304]{1,0:T(8,128)(2,1)} %param.10) | copy-start | bytes 1769476
  119.7 56.5 %copy-start.9 = (f32[2304]{0:T(1024)S(1)}, f32[2304]{0:T(1024)}, u32[]{:S(2)}) copy-start(f32[2304]{0:T(1024)} %param.12) | copy-start | bytes 27652
  119.7 58.7 %copy-start.10 = (s32[128,2]{0,1:T(2,128)S(1)}, s32[128,2]{0,1:T(2,128)}, u32[]{:S(2)}) copy-start(s32[128,2]{0,1:T(2,128)} %param.19) | copy-start | bytes 3076
  119.8 113.4 %copy-start.6 = (f32[2304,8]{0,1:T(8,128)S(1)}, f32[2304,8]{0,1:T(8,128)}, u32[]{:S(2)}) copy-start(f32[2304,8]{0,1:T(8,128)} %param.15) | copy-start | bytes 221188
  119.8 108.8 %all-gather.8.cloned.1.call-start = ((), (), s32[]{:S(2)}) async-start(), calls=%async_computation.5 | async-start | bytes 5308416 | tf_op jit(solution)/shard_map/all_gather | solution.py:168
  178.4 152.1 %reduce-scatter.5.cloned.1.call-start = ((), (), s32[]{:S(2)}) async-start(), calls=%async_computation.6 | async-start | bytes 5308416 | tf_op jit(solution)/shard_map/reduce_scatter | solution.py:198
  231.7 1.5 copy-start.3
  271.2 61.4 %copy-start.1 = (bf16[3,2304,64]{1,2,0:T(8,128)(2,1)S(1)}, bf16[3,2304,64]{1,2,0:T(8,128)(2,1)}, u32[]{:S(2)}) copy-start(bf16[3,2304,64]{1,2,0:T(8,128)(2,1)} %param.13) | copy-start | bytes 2654212
  271.2 59.3 %copy-start.5 = (bf16[128,2304]{1,0:T(8,128)(2,1)S(1)}, bf16[128,2304]{1,0:T(8,128)(2,1)}, u32[]{:S(2)}) copy-start(bf16[128,2304]{1,0:T(8,128)(2,1)} %reduce-scatter.3.cloned.1.call-done) | copy-start | bytes 1769476
Sparse Core Ops, SparseCore 0:
  10.8 54.3 all-gather.3
  70.8 25.4 all-gather.5
  119.9 54.9 reduce-scatter.2
  178.5 50.0 all-gather.7
  276.7 53.7 reduce-scatter.4
where the time goes:
time: 340 us; the launch traced here: 339 us
  waiting for transfers between devices  220 us (65%)
  matrix products  67.4 us (20%)
  blocking collectives  17.3 us (5%)
  other arithmetic  16.9 us (5%)
  between operations  14 us (4%)
    reduce_scatter x1, waiting for transfers between devices, shards(): lax.psum_scatter(jnp.dot(attended, w_out, preferred_element_type=jnp.floa...  54.9 us
    all_gather x1, waiting for transfers between devices, shards(): lax.all_gather(normed, 'tensor', axis=0, tiled=True)  54.5 us
    reduce_scatter x1, waiting for transfers between devices, shards(): lax.psum_scatter(placed.astype(jnp.bfloat16), 'tensor', scatter_dimension...  53.1 us
    all_gather x1, waiting for transfers between devices, shards(): lax.all_gather(normed_ffn, 'tensor', axis=0, tiled=True)  40.4 us
    dot_general x1, matrix products, expert_apply(): output = jnp.dot(hidden_act, w_down, preferred_element_type=jnp.float32)  23.2 us
    all_gather x1, waiting for transfers between devices, shards(): lax.all_gather(kv_rows, 'seq', axis=0, tiled=True)  17.4 us
    dot_general x1, matrix products, expert_apply(): lax.dot_general(slot_rows, w_gate_up[0], contract, preferred_element_type...  12.5 us
    all_gather x1, blocking collectives, shards(): lax.all_gather(expert_ids, 'tensor', axis=0, tiled=True)  9.15 us
  transfers between devices with their start and end apart: 5, of which 5 were waited for; matrix products, arithmetic and copies ran while one was open for 0% of the time, Pallas kernels for 0%

commit v1 on v0

--- a/solution.py
+++ b/solution.py
@@ -7,6 +7,19 @@
 HD = 64
 epsilon = 1e-06
 low_score = -1e30
+
+
+def gather_around(shard, axis, dim):
+    ways = lax.axis_size(axis)
+    up = [(d, (d + 1) % ways) for d in range(ways)]
+    down = [(d, (d - 1) % ways) for d in range(ways)]
+    earlier, later = ([shard], [shard])
+    for _ in range(ways // 2):
+        earlier.append(lax.ppermute(earlier[-1], axis, up))
+    for _ in range((ways - 1) // 2):
+        later.append(lax.ppermute(later[-1], axis, down))
+    line = jnp.concatenate([*earlier[::-1], *later[1:]], axis=dim)
+    return jnp.roll(line, (lax.axis_index(axis) - ways // 2) * shard.shape[dim], axis=dim)
 
 
 def rms_norm(hidden_rows, gain):
@@ -165,7 +178,7 @@
     own_expert = tensor_place // slice_count
     slot_count = local_rows // 2
     full_rows, full_ids = (
-        lax.all_gather(normed_ffn, "tensor", axis=0, tiled=True),
+        gather_around(normed_ffn, "tensor", 0),
         lax.all_gather(expert_ids, "tensor", axis=0, tiled=True),
     )
     block_ids = full_ids.reshape(tensor_count, local_rows, 2)

time: 340 us -> 358 us (1.053)
  starting transfers between devices: 0.39 us -> 8.92 us
  local copies, waits for them, and re-layouts: 2.76 us -> 10.1 us
  blocking collectives: 17.3 us -> 20.9 us
    all_gather x1 -> x0, waiting for transfers between devices: 40.4 us -> none  [shards(): lax.all_gather(normed_ffn, 'tensor', axis=0, tiled=True)]
    ppermute x0 -> x7, waiting for transfers between devices: none -> 39.5 us  [the longest x4 22.4 us: gather_around(): earlier.append(lax.ppermute(earlier[-1], axis, up))]
    ppermute x0 -> x7, starting transfers between devices: none -> 8.76 us  [the longest x3 8.69 us: gather_around(): later.append(lax.ppermute(later[-1], axis, down))]
    unnamed x25 -> x40, local copies, waits for them, and re-layouts: 2.36 us -> 9.35 us
    all_gather x1, blocking collectives: 9.15 us -> 12.8 us  [shards(): lax.all_gather(expert_ids, 'tensor', axis=0, tiled=True)]
  transfers between devices with their start and end apart: 5 -> 11, of which waited for: 5 -> 8; matrix products, arithmetic and copies ran while one was open for 0% -> 1% of each run, Pallas kernels for 0% -> 0%
where the time goes in v1:
time: 358 us; the launch traced here: 357 us
  waiting for transfers between devices  222 us (62%)
  matrix products  65.1 us (18%)
  blocking collectives  20.9 us (6%)
  other arithmetic  16.1 us (4%)
  between operations  14.1 us (4%)
  local copies, waits for them, and re-layouts  10.1 us (3%)
  starting transfers between devices  8.92 us (2%)
    reduce_scatter x1, waiting for transfers between devices, shards(): lax.psum_scatter(placed.astype(jnp.bfloat16), 'tensor', scatter_dimension...  55.5 us
    reduce_scatter x1, waiting for transfers between devices, shards(): lax.psum_scatter(jnp.dot(attended, w_out, preferred_element_type=jnp.floa...  55.1 us
    all_gather x1, waiting for transfers between devices, shards(): lax.all_gather(normed, 'tensor', axis=0, tiled=True)  54.5 us
    dot_general x1, matrix products, expert_apply(): output = jnp.dot(hidden_act, w_down, preferred_element_type=jnp.float32)  23.3 us
    ppermute x4, waiting for transfers between devices, gather_around(): earlier.append(lax.ppermute(earlier[-1], axis, up))  22.4 us
    all_gather x1, waiting for transfers between devices, shards(): lax.all_gather(kv_rows, 'seq', axis=0, tiled=True)  17.4 us
    ppermute x3, waiting for transfers between devices, gather_around(): later.append(lax.ppermute(later[-1], axis, down))  17.1 us
    all_gather x1, blocking collectives, shards(): lax.all_gather(expert_ids, 'tensor', axis=0, tiled=True)  12.8 us
  transfers between devices with their start and end apart: 11, of which 8 were waited for; matrix products, arithmetic and copies ran while one was open for 1% of the time, Pallas kernels for 0%

profile of v1, /device:TPU:0, one launch (start us, length us, event | category | flops | bytes accessed | tf_op | source)
XLA Modules:
  0.0 357.3 jit_solution(2976614681670291241)
XLA Ops:
  7.2 0.0 copy-start
  7.2 0.0 all-gather.3.cloned.1.call-start
  7.2 1.3 fusion.20
  8.6 2.1 fusion.22
  10.7 0.0 all-gather.3.cloned.1.call-update
  10.7 0.0 all-gather.5.cloned.1.call-start
  10.8 54.5 %all-gather.3.cloned.1.call-done = bf16[1024,2304]{1,0:T(8,128)(2,1)} async-done(((bf16[128,2304]{1,0:T(8,128)(2,1)}), bf16[1024,2304]{1,0:T(8,128)(2,1)}) %all-gather.3.cloned.1.call-update) | async-done | bytes 4718608 | tf_op jit(solution)/shard_map/all_gather | solution.py:133
  65.3 4.0 %fusion.95 = f32[1024,192]{0,1:S(1)} fusion(bf16[1024,2304]{1,0:T(8,128)(2,1)} %all-gather.3.cloned.1.call-done, bf16[2304,192]{0,1:T(8,128)(2,1)S(1)} %bitcast.62), kind=kOutput, calls=%fused_computation.137 | convolution fusion | flops 905969664 | bytes 6389760
  69.3 0.6 fusion.70
  69.9 0.8 fusion.93
  70.6 0.0 all-gather.5.cloned.1.call-update
  70.7 0.0 reduce-scatter.3.cloned.1.call-start
  70.7 8.1 %all_gather.12 = s32[4096]{0:T(1024)S(1)} all-gather(s32[1024]{0:T(1024)S(1)} %copy-done.8), channel_id=1, replica_groups=mesh['seq'=4,'tensor'=8] {'seq'}, dimensions={0}, use_global_device_ids=true | all-gather | bytes 20480 | tf_op jit(solution)/shard_map/all_gather | solution.py:158
  78.9 17.4 %all-gather.5.cloned.1.call-done = bf16[4096,1,128]{0,2,1:T(8,128)(2,1)} async-done(((bf16[1024,1,128]{0,2,1:T(8,128)(2,1)}), bf16[4096,1,128]{0,2,1:T(8,128)(2,1)}) %all-gather.5.cloned.1.call-update) | async-done | bytes 1048592 | tf_op jit(solution)/shard_map/all_gather | solution.py:157
  96.3 2.3 fusion.41
  98.6 4.1 %fusion.8 = (f32[1024]{0:T(1024)S(1)}, f32[1024]{0:T(1024)S(1)}, f32[1024,2048]{1,0:T(8,128)S(1)}) fusion(s32[2048]{0:T(1024)S(1)} %iota_add_fusion, s32[2048]{0:T(1024)S(1)} %get-tuple-element.23, s32[1024]{0:T(1024)S(1)} %iota_add_fusion.1, s32[1024]{0:T(1024)S(1)} %copy-done.8, f32[1024,2048]{1,0:T(8,128)S(1)} %fusion.41, ...), kind=kOutput, calls=%fused_computation.14 | convolution fusion | flops 293861376 | bytes 17211392 | tf_op jit(solution)/shard_map/qhd,khd->hqk/dot_general | solution.py:59
  102.7 6.2 %fusion.12 = (f32[1024]{0:T(1024)S(1)}, f32[1024]{0:T(1024)S(1)}) fusion(f32[1024,2048]{1,0:T(8,128)S(1)} %fusion.41, f32[1024]{0:T(1024)S(1)} %get-tuple-element.26, s32[2048]{0:T(1024)S(1)} %get-tuple-element.22, s32[1024]{0:T(1024)S(1)} %iota_add_fusion.1, s32[1024]{0:T(1024)S(1)} %copy-done.8, f32[1024]{0:T(1024)S(1)} %get-tuple-element.25, ...), kind=kLoop, calls=%fused_computation.21 | loop fusion | flops 33552384 | bytes 16826368 | tf_op jit(solution)/shard_map/reduce_sum | solution.py:69
  108.9 0.0 copy-start.11
  108.9 2.8 fusion.29
  111.7 0.0 copy-start.2
  111.7 0.0 copy-start.9
  111.7 0.0 copy-start.10
  111.7 8.0 %convolution_convert_fusion.1 = bf16[1024,2304]{1,0:T(8,128)(2,1)} fusion(bf16[64,2304]{1,0:T(8,128)(2,1)S(1)} %copy-done.11, f32[1024,64]{0,1:T(8,128)S(1)} %fusion.29, f32[1024,2048]{1,0:T(8,128)} %copy-done.4, f32[1024]{0:T(1024)S(1)} %get-tuple-element.25, s32[2048]{0:T(1024)S(1)} %iota_add_fusion, s32[2048]{0:T(1024)S(1)} %get-tuple-element.23, ...), kind=kOutput, calls=%fused_computation.17 | convolution fusion | flops 589758464 | bytes 13959168 | tf_op jit(solution)/shard_map/dot_general | solution.py:169
  119.8 0.0 reduce-scatter.3.cloned.1.call-update
  119.8 0.0 reduce-scatter.5.cloned.1.call-start
  119.8 55.1 %reduce-scatter.3.cloned.1.call-done = bf16[128,2304]{1,0:T(8,128)(2,1)} async-done(((bf16[1024,2304]{1,0:T(8,128)(2,1)}), bf16[128,2304]{1,0:T(8,128)(2,1)}) %reduce-scatter.3.cloned.1.call-update) | async-done | bytes 589840 | tf_op jit(solution)/shard_map/reduce_scatter | solution.py:168
  174.9 1.3 multiply_reduce_fusion
  176.3 1.3 multiply_convert_fusion.1
  177.5 0.1 collective-permute-start
  177.6 11.1 %collective-permute-done = bf16[128,2304]{1,0:T(8,128)(2,1)S(1)} collective-permute-done((bf16[128,2304]{1,0:T(8,128)(2,1)S(1)}, bf16[128,2304]{1,0:T(8,128)(2,1)S(1)}, u32[]{:S(2)}, u32[]{:S(2)}) %collective-permute-start) | collective-permute-done | bytes 589856 | tf_op jit(solution)/shard_map/ppermute | solution.py:18
  188.7 0.0 collective-permute-start.1
  188.7 3.5 collective-permute-start.4
  192.3 11.3 %collective-permute-done.1 = bf16[128,2304]{1,0:T(8,128)(2,1)S(1)} collective-permute-done((bf16[128,2304]{1,0:T(8,128)(2,1)S(1)}, bf16[128,2304]{1,0:T(8,128)(2,1)S(1)}, u32[]{:S(2)}, u32[]{:S(2)}) %collective-permute-start.1) | collective-permute-done | bytes 589856 | tf_op jit(solution)/shard_map/ppermute | solution.py:18
  203.6 0.0 collective-permute-start.2
  203.6 12.8 %all_gather.15 = s32[1024,2]{0,1:T(2,128)S(1)} all-gather(s32[128,2]{0,1:T(2,128)S(1)} %copy-done.10), channel_id=1, replica_groups=mesh['seq'=4,'tensor'=8] {'tensor'}, dimensions={0}, use_global_device_ids=true | all-gather | bytes 9216 | tf_op jit(solution)/shard_map/all_gather | solution.py:182
  216.5 1.3 collective-permute-start.5
  217.9 0.2 select_reduce_fusion
  218.1 0.2 fusion.77
  218.3 0.1 eq.94
  218.4 12.9 %collective-permute-done.5 = bf16[128,2304]{1,0:T(8,128)(2,1)} collective-permute-done((bf16[128,2304]{1,0:T(8,128)(2,1)S(1)}, bf16[128,2304]{1,0:T(8,128)(2,1)}, u32[]{:S(2)}, u32[]{:S(2)}) %collective-permute-start.5) | collective-permute-done | bytes 589856 | tf_op jit(solution)/shard_map/ppermute | solution.py:20
  231.2 3.8 %collective-permute-start.6 = (bf16[128,2304]{1,0:T(8,128)(2,1)}, bf16[128,2304]{1,0:T(8,128)(2,1)S(1)}, u32[]{:S(2)}, u32[]{:S(2)}) collective-permute-start(bf16[128,2304]{1,0:T(8,128)(2,1)} %collective-permute-done.5), channel_id=1, source_target_pairs={{0,7},{1,0},{2,1},{3,2},{4,3},{5,4},{6,5},{7,6},{8,15},{9,8},{10,9... | collective-permute-start | bytes 1769480 | tf_op jit(solution)/shard_map/ppermute | solution.py:20
  235.0 1.1 constant_dynamic-update-slice_fusion.15
  236.1 1.1 constant_dynamic-update-slice_fusion.14
  237.4 1.1 constant_dynamic-update-slice_fusion.9
  238.6 4.2 %collective-permute-done.6 = bf16[128,2304]{1,0:T(8,128)(2,1)S(1)} collective-permute-done((bf16[128,2304]{1,0:T(8,128)(2,1)}, bf16[128,2304]{1,0:T(8,128)(2,1)S(1)}, u32[]{:S(2)}, u32[]{:S(2)}) %collective-permute-start.6) | collective-permute-done | bytes 589856 | tf_op jit(solution)/shard_map/ppermute | solution.py:20
  242.8 1.1 constant_dynamic-update-slice_fusion.7
  243.9 1.1 constant_dynamic-update-slice_fusion.6
  245.2 1.1 constant_dynamic-update-slice_fusion.1
  246.4 0.0 copy-start.6
  246.4 0.3 constant_dynamic-slice_fusion
  246.7 0.8 convolution_convert_fusion.2
  247.5 1.5 copy-done.3
  248.9 1.9 fusion.96
  250.9 0.1 reduce_sum.80
  251.0 0.1 sub.89
  251.1 12.5 %fusion.2 = f32[512,2880]{0,1:T(8,128)} fusion(bf16[512,2304]{1,0:T(8,128)(2,1)} %bitcast.66, bf16[2,2880,2304]{2,1,0:T(8,128)(2,1)} %param.16), kind=kOutput, calls=%fused_computation.2 | convolution fusion | flops 6794772480 | bytes 21528576 | tf_op jit(solution)/shard_map/dot_general | solution.py:102
  263.6 0.1 div.37
  263.7 0.1 mul.197
  263.8 23.3 %fusion.11 = bf16[512,2304]{1,0:T(8,128)(2,1)} fusion(bf16[2880,2304]{1,0:T(8,128)(2,1)} %param.17, f32[512]{0:T(512)S(1)} %mul.197, f32[512,2880]{0,1:T(8,128)} %fusion.2, bf16[512,2304]{1,0:T(8,128)(2,1)} %bitcast.67, bf16[2,2880,2304]{2,1,0:T(8,128)(2,1)} %param.16), kind=kOutput, calls=%fused_computation.20 | convolution fusion | flops 13600751616 | bytes 37160960 | tf_op jit(solution)/shard_map/dot_general | solution.py:107
  287.1 5.3 %convolution_convert_fusion = bf16[8,128,2304]{2,1,0:T(8,128)(2,1)} fusion(bf16[8,64,2304]{2,1,0:T(8,128)(2,1)} %bitcast.68, s32[8,128]{1,0:T(8,128)S(1)} %broadcast_add_fusion, pred[8,128]{1,0:T(8,128)(4,1)S(1)} %broadcast_compare_fusion), kind=kOutput, calls=%fused_computation.16 | convolution fusion | flops 304480256 | bytes 7083008 | tf_op jit(solution)/shard_map/sjr,sjd->srd/dot_general | solution.py:205
  292.3 0.0 reduce-scatter.5.cloned.1.call-update
  292.4 0.8 copy.26
  293.2 55.5 %reduce-scatter.5.cloned.1.call-done = bf16[128,2304]{1,0:T(8,128)(2,1)} async-done(((bf16[1024,2304]{1,0:T(8,128)(2,1)}), bf16[128,2304]{1,0:T(8,128)(2,1)}) %reduce-scatter.5.cloned.1.call-update) | async-done | bytes 589840 | tf_op jit(solution)/shard_map/reduce_scatter | solution.py:211
  348.7 2.1 add_convert_fusion
  (51 shorter events, 0.7 us)
Async XLA Ops:
  7.2 58.1 %copy-start = (bf16[3,2304,64]{1,2,0:T(8,128)(2,1)S(1)}, bf16[3,2304,64]{1,2,0:T(8,128)(2,1)}, u32[]{:S(2)}) copy-start(bf16[3,2304,64]{1,2,0:T(8,128)(2,1)} %param.13) | copy-start | bytes 2654212
  7.2 63.5 %copy-start.8 = (s32[1024]{0:T(1024)S(1)}, s32[1024]{0:T(1024)}, u32[]{:S(2)}) copy-start(s32[1024]{0:T(1024)} %param.18) | copy-start | bytes 12292
  7.2 58.1 %all-gather.3.cloned.1.call-start = ((), (), s32[]{:S(2)}) async-start(), calls=%async_computation.2 | async-start | bytes 5308416 | tf_op jit(solution)/shard_map/all_gather | solution.py:133
  10.7 85.6 %all-gather.5.cloned.1.call-start = ((), (), s32[]{:S(2)}) async-start(), calls=%async_computation.3 | async-start | bytes 1310720 | tf_op jit(solution)/shard_map/all_gather | solution.py:157
  70.7 104.2 %reduce-scatter.3.cloned.1.call-start = ((), (), s32[]{:S(2)}) async-start(), calls=%async_computation.4 | async-start | bytes 5308416 | tf_op jit(solution)/shard_map/reduce_scatter | solution.py:168
  96.3 2.3 copy-start.7
  102.7 6.2 %copy-start.4 = (f32[1024,2048]{1,0:T(8,128)}, f32[1024,2048]{1,0:T(8,128)S(1)}, u32[]{:S(2)}) copy-start(f32[1024,2048]{1,0:T(8,128)S(1)} %get-tuple-element.27) | copy-start | bytes 25165828
  108.9 2.8 copy-start.11
  111.7 63.2 %copy-start.2 = (bf16[128,2304]{1,0:T(8,128)(2,1)S(1)}, bf16[128,2304]{1,0:T(8,128)(2,1)}, u32[]{:S(2)}) copy-start(bf16[128,2304]{1,0:T(8,128)(2,1)} %param.10) | copy-start | bytes 1769476
  111.7 64.6 %copy-start.9 = (f32[2304]{0:T(1024)S(1)}, f32[2304]{0:T(1024)}, u32[]{:S(2)}) copy-start(f32[2304]{0:T(1024)} %param.12) | copy-start | bytes 27652
  111.7 91.9 %copy-start.10 = (s32[128,2]{0,1:T(2,128)S(1)}, s32[128,2]{0,1:T(2,128)}, u32[]{:S(2)}) copy-start(s32[128,2]{0,1:T(2,128)} %param.19) | copy-start | bytes 3076
  119.8 228.9 %reduce-scatter.5.cloned.1.call-start = ((), (), s32[]{:S(2)}) async-start(), calls=%async_computation.5 | async-start | bytes 5308416 | tf_op jit(solution)/shard_map/reduce_scatter | solution.py:211
  177.5 11.2 %collective-permute-start = (bf16[128,2304]{1,0:T(8,128)(2,1)S(1)}, bf16[128,2304]{1,0:T(8,128)(2,1)S(1)}, u32[]{:S(2)}, u32[]{:S(2)}) collective-permute-start(bf16[128,2304]{1,0:T(8,128)(2,1)S(1)} %multiply_convert_fusion.1), channel_id=1, source_target_pairs={{0,1},{1,2},{2,3},{3,4},{4,5},{5,6},{6,7},{7,0},{8,9},{9,10},{10,1... | collective-permute-start | bytes 1769480 | tf_op jit(solution)/shard_map/ppermute | solution.py:18
  188.7 14.9 %collective-permute-start.1 = (bf16[128,2304]{1,0:T(8,128)(2,1)S(1)}, bf16[128,2304]{1,0:T(8,128)(2,1)S(1)}, u32[]{:S(2)}, u32[]{:S(2)}) collective-permute-start(bf16[128,2304]{1,0:T(8,128)(2,1)S(1)} %collective-permute-done), channel_id=1, source_target_pairs={{0,1},{1,2},{2,3},{3,4},{4,5},{5,6},{6,7},{7,0},{8,9},{9,10},{10,1... | collective-permute-start | bytes 1769480 | tf_op jit(solution)/shard_map/ppermute | solution.py:18
  188.7 27.7 %collective-permute-start.4 = (bf16[128,2304]{1,0:T(8,128)(2,1)S(1)}, bf16[128,2304]{1,0:T(8,128)(2,1)S(1)}, u32[]{:S(2)}, u32[]{:S(2)}) collective-permute-start(bf16[128,2304]{1,0:T(8,128)(2,1)S(1)} %multiply_convert_fusion.1), channel_id=1, source_target_pairs={{0,7},{1,0},{2,1},{3,2},{4,3},{5,4},{6,5},{7,6},{8,15},{9,8},{10,9... | collective-permute-start | bytes 1769480 | tf_op jit(solution)/shard_map/ppermute | solution.py:20
  203.6 14.2 %collective-permute-start.2 = (bf16[128,2304]{1,0:T(8,128)(2,1)S(1)}, bf16[128,2304]{1,0:T(8,128)(2,1)}, u32[]{:S(2)}, u32[]{:S(2)}) collective-permute-start(bf16[128,2304]{1,0:T(8,128)(2,1)S(1)} %collective-permute-done.1), channel_id=1, source_target_pairs={{0,1},{1,2},{2,3},{3,4},{4,5},{5,6},{6,7},{7,0},{8,9},{9,10},{10,1... | collective-permute-start | bytes 1769480 | tf_op jit(solution)/shard_map/ppermute | solution.py:18
  216.5 14.8 %collective-permute-start.5 = (bf16[128,2304]{1,0:T(8,128)(2,1)S(1)}, bf16[128,2304]{1,0:T(8,128)(2,1)}, u32[]{:S(2)}, u32[]{:S(2)}) collective-permute-start(bf16[128,2304]{1,0:T(8,128)(2,1)S(1)} %collective-permute-done.4), channel_id=1, source_target_pairs={{0,7},{1,0},{2,1},{3,2},{4,3},{5,4},{6,5},{7,6},{8,15},{9,8},{10,9... | collective-permute-start | bytes 1769480 | tf_op jit(solution)/shard_map/ppermute | solution.py:20
  217.8 17.2 %collective-permute-start.3 = (bf16[128,2304]{1,0:T(8,128)(2,1)}, bf16[128,2304]{1,0:T(8,128)(2,1)}, u32[]{:S(2)}, u32[]{:S(2)}) collective-permute-start(bf16[128,2304]{1,0:T(8,128)(2,1)} %collective-permute-done.2), channel_id=1, source_target_pairs={{0,1},{1,2},{2,3},{3,4},{4,5},{5,6},{6,7},{7,0},{8,9},{9,10},{10,1... | collective-permute-start | bytes 1769480 | tf_op jit(solution)/shard_map/ppermute | solution.py:18
  231.2 11.5 %collective-permute-start.6 = (bf16[128,2304]{1,0:T(8,128)(2,1)}, bf16[128,2304]{1,0:T(8,128)(2,1)S(1)}, u32[]{:S(2)}, u32[]{:S(2)}) collective-permute-start(bf16[128,2304]{1,0:T(8,128)(2,1)} %collective-permute-done.5), channel_id=1, source_target_pairs={{0,7},{1,0},{2,1},{3,2},{4,3},{5,4},{6,5},{7,6},{8,15},{9,8},{10,9... | collective-permute-start | bytes 1769480 | tf_op jit(solution)/shard_map/ppermute | solution.py:20
  246.4 2.6 copy-start.6
  247.5 1.5 copy-start.3
  263.8 87.0 %copy-start.1 = (bf16[3,2304,64]{1,2,0:T(8,128)(2,1)S(1)}, bf16[3,2304,64]{1,2,0:T(8,128)(2,1)}, u32[]{:S(2)}) copy-start(bf16[3,2304,64]{1,2,0:T(8,128)(2,1)} %param.13) | copy-start | bytes 2654212
  287.1 61.6 %copy-start.5 = (bf16[128,2304]{1,0:T(8,128)(2,1)S(1)}, bf16[128,2304]{1,0:T(8,128)(2,1)}, u32[]{:S(2)}) copy-start(bf16[128,2304]{1,0:T(8,128)(2,1)} %reduce-scatter.3.cloned.1.call-done) | copy-start | bytes 1769476
Sparse Core Ops, SparseCore 0:
  10.8 54.3 all-gather.2
  70.8 25.4 all-gather.4
  119.9 54.9 reduce-scatter.2
  292.5 56.1 reduce-scatter.4
